TPU v7x, 32 devices: a whole 2x2x4 slice. The times are simulated.
32 devices in a mesh: dp: 4 (over y, x), ctx: 8 (over z, core).
Axes of the slice: x: 2, y: 2, z: 4, core: 2. Of those that a mesh axis runs over, the one named last changes fastest.
Arguments:
- queries: bfloat16 [4, 2048, 512], P('dp', 'ctx'), may hold values from -6 to 6
- key_vectors: bfloat16 [4, 2048, 512], P('dp', 'ctx'), may hold values from -6 to 6
- value_vectors: bfloat16 [4, 2048, 512], P('dp', 'ctx'), may hold values from -6 to 6
- grad_output: bfloat16 [4, 2048, 512], P('dp', 'ctx'), may hold values from -768 to 768
- pattern: int32 [4, 16, 2], P('dp', 'ctx'), may hold values from 0 to 1
- lengths: int32 [4, 1], P('dp'), may hold values from 512 to 2048, as said below
- widths: int32 [4, 1], P('dp'), may hold values from 1 to 2, as said below
- relative_bucket_bias: float32 [4, 7], replicated, may hold values from -4 to 4
Outputs:
- grad_queries: bfloat16 [4, 2048, 512], P('dp', 'ctx')
- grad_keys: bfloat16 [4, 2048, 512], P('dp', 'ctx')
- value_row_gradients: bfloat16 [4, 2048, 512], P('dp', 'ctx')
- grad_bias: float32 [4, 7], replicated
Inputs may be any that keep to these rules, and one draw needn't show every extreme that they name: `lengths`: one user has a history of all 2048 events and one has 512. `widths`: some user has the widest band and some the narrowest.
All inputs are finite; a program needn't handle non-finite values.
Results may differ from a plain program's by a relative error of at most 0.005.
Values may be sent and summed in bfloat16 or wider, within the bound.
A program may use at most 64 MiB of HBM per device.

v0:
```python
import jax
import jax.numpy as jnp
from jax import lax
from jax.sharding import PartitionSpec as P

BLOCK = 128
GROUP = 8
FAR = 2
NBUCK = 7
SEQ = 2048


def from_behind(array, axis, by):
    size = lax.axis_size(axis)
    pairs = [(i, i + by) for i in range(size) if 0 <= i + by < size]
    return lax.ppermute(array, axis, pairs)


def tile_grads(q_rows, g_rows, k_rows, v_rows, keep_mask, buckets, relative_bucket_bias):
    groups, query_len, model_width = q_rows.shape
    key_len = k_rows.shape[1]
    head_count = relative_bucket_bias.shape[0]
    head_dim = model_width // head_count
    q_blocks = query_len // BLOCK
    k_blocks = key_len // BLOCK
    scaling = head_dim ** (-0.5)
    q_heads = q_rows.reshape(groups, query_len, head_count, head_dim)
    g_heads = g_rows.reshape(groups, query_len, head_count, head_dim)
    k_heads = k_rows.reshape(groups, key_len, head_count, head_dim)
    v_heads = v_rows.reshape(groups, key_len, head_count, head_dim)
    onehot = (buckets[..., None] == jnp.arange(NBUCK, dtype=jnp.int32)).astype(jnp.float32)
    bias_tile = jnp.einsum(
        "gxyu,hu->ghxy", onehot, relative_bucket_bias, precision=lax.Precision.HIGHEST
    )
    raw_score = jnp.einsum("gqhd,gkhd->ghqk", q_heads, k_heads, preferred_element_type=jnp.float32)
    score = (raw_score * scaling).reshape(groups, head_count, q_blocks, BLOCK, k_blocks, BLOCK)
    score = (score + bias_tile[:, :, :, None, :, None]).reshape(
        groups, head_count, query_len, key_len
    )
    keep = keep_mask[:, None, :, :]
    sigmoid_s = jax.nn.sigmoid(score)
    weights_bf = jnp.where(keep, score * sigmoid_s / SEQ, 0.0).astype(jnp.bfloat16)
    value_gradient = jnp.einsum(
        "ghqk,gqhd->gkhd", weights_bf, g_heads, preferred_element_type=jnp.float32
    )
    grad_prob = jnp.einsum("gqhd,gkhd->ghqk", g_heads, v_heads, preferred_element_type=jnp.float32)
    dscore = jnp.where(keep, grad_prob * (sigmoid_s * (1.0 + score * (1.0 - sigmoid_s))) / SEQ, 0.0)
    dscore_bf = dscore.astype(jnp.bfloat16)
    block_sums = dscore.reshape(groups, head_count, q_blocks, BLOCK, k_blocks, BLOCK).sum(
        axis=(3, 5)
    )
    grad_bias = jnp.einsum("ghxy,gxyu->hu", block_sums, onehot, precision=lax.Precision.HIGHEST)
    grad_q = (
        jnp.einsum("ghqk,gkhd->gqhd", dscore_bf, k_heads, preferred_element_type=jnp.float32)
        * scaling
    )
    key_gradient = (
        jnp.einsum("ghqk,gqhd->gkhd", dscore_bf, q_heads, preferred_element_type=jnp.float32)
        * scaling
    )
    return (
        grad_q.reshape(groups, query_len, model_width),
        key_gradient.reshape(groups, key_len, model_width),
        value_gradient.reshape(groups, key_len, model_width),
        grad_bias,
    )


def local_mask(span_id, length, band_width, token_count):
    blocks = token_count // BLOCK
    places = span_id * token_count + jnp.arange(token_count, dtype=jnp.int32)
    block_ids = jnp.arange(token_count, dtype=jnp.int32) // BLOCK
    allowed = (block_ids[:, None] - block_ids[None, :] <= band_width) & (
        places[None, :] <= places[:, None]
    )
    allowed = allowed & (places[:, None] < length) & (places[None, :] < length)
    grid = jnp.arange(blocks, dtype=jnp.int32)
    buckets = jnp.clip(grid[:, None] - grid[None, :], 0, NBUCK - 1)
    return (allowed[None], buckets[None])


def near_mask(span_id, length, band_width, token_count):
    blocks = token_count // BLOCK
    q_places = span_id * token_count + jnp.arange(token_count, dtype=jnp.int32)
    k_places = (span_id - 1) * token_count + jnp.arange(token_count, dtype=jnp.int32)
    block_ids = jnp.arange(token_count, dtype=jnp.int32) // BLOCK
    distance = block_ids[:, None] + blocks - block_ids[None, :]
    allowed = (distance <= band_width) & (q_places[:, None] < length) & (k_places[None, :] < length)
    allowed = allowed & (span_id >= 1) & (span_id < GROUP)
    grid = jnp.arange(blocks, dtype=jnp.int32)
    buckets = jnp.clip(grid[:, None] + blocks - grid[None, :], 0, NBUCK - 1)
    return (allowed[None], buckets[None])


def far_mask(span_id, chosen, distance, length, token_count):
    blocks = token_count // BLOCK
    grid = jnp.arange(blocks, dtype=jnp.int32)
    inner = jnp.arange(BLOCK, dtype=jnp.int32)
    q_places = span_id * token_count + grid[:, None] * BLOCK + inner[None, :]
    k_places = (span_id - distance) * token_count + chosen[:, None] * BLOCK + inner[None, :]
    allowed = (q_places[:, :, None] < length) & (k_places[:, None, :] < length)
    allowed = allowed & (span_id >= distance) & (span_id < GROUP)
    buckets = jnp.clip(distance * blocks + grid - chosen, 0, NBUCK - 1)[:, None, None]
    return (allowed, buckets)


def local_terms(q_rows, g_rows, k_rows, v_rows, span_id, length, band_width, relative_bucket_bias):
    keep_mask, buckets = local_mask(span_id, length, band_width, q_rows.shape[0])
    grads = tile_grads(
        q_rows[None],
        g_rows[None],
        k_rows[None],
        v_rows[None],
        keep_mask,
        buckets,
        relative_bucket_bias,
    )
    return (grads[0][0], grads[1][0], grads[2][0], grads[3])


def near_terms(q_rows, g_rows, k_rows, v_rows, span_id, length, band_width, relative_bucket_bias):
    keep_mask, buckets = near_mask(span_id, length, band_width, q_rows.shape[0])
    grads = tile_grads(
        q_rows[None],
        g_rows[None],
        k_rows[None],
        v_rows[None],
        keep_mask,
        buckets,
        relative_bucket_bias,
    )
    return (grads[0][0], grads[1][0], grads[2][0], grads[3])


def far_terms(
    q_rows, g_rows, k_rows, v_rows, chosen, span_id, distance, length, relative_bucket_bias
):
    token_count, model_width = q_rows.shape
    blocks = token_count // BLOCK
    keep_mask, buckets = far_mask(span_id, chosen, distance, length, token_count)
    q_tiles = q_rows.reshape(blocks, BLOCK, model_width)
    g_tiles = g_rows.reshape(blocks, BLOCK, model_width)
    k_tiles = jnp.take(k_rows.reshape(blocks, BLOCK, model_width), chosen, axis=0)
    v_tiles = jnp.take(v_rows.reshape(blocks, BLOCK, model_width), chosen, axis=0)
    grad_q, key_gradient, value_gradient, grad_bias = tile_grads(
        q_tiles, g_tiles, k_tiles, v_tiles, keep_mask, buckets, relative_bucket_bias
    )
    selector_matrix = (chosen[:, None] == jnp.arange(blocks, dtype=jnp.int32)[None, :]).astype(
        jnp.float32
    )
    key_gradient = jnp.einsum(
        "as,apc->spc", selector_matrix, key_gradient, precision=lax.Precision.HIGHEST
    ).reshape(token_count, model_width)
    value_gradient = jnp.einsum(
        "as,apc->spc", selector_matrix, value_gradient, precision=lax.Precision.HIGHEST
    ).reshape(token_count, model_width)
    return (grad_q.reshape(token_count, model_width), key_gradient, value_gradient, grad_bias)


def on_device(
    queries, key_vectors, value_vectors, grad_output, pattern, lengths, widths, relative_bucket_bias
):
    position = lax.axis_index("ctx")
    span_id = position % GROUP
    user_slot = position // GROUP
    length = lengths[0, user_slot]
    band_width = widths[0, user_slot]
    q_rows = queries[0]
    k_rows = key_vectors[0]
    v_rows = value_vectors[0]
    g_rows = grad_output[0]
    block_table = pattern[0]
    grad_q, key_gradient, value_gradient, grad_bias = local_terms(
        q_rows, g_rows, k_rows, v_rows, span_id, length, band_width, relative_bucket_bias
    )
    distances = [2**section for section in range(FAR + 1)]
    table_bf = block_table.astype(jnp.bfloat16)
    for section, distance in enumerate(distances):
        far_q, far_g, far_table = from_behind((q_rows, g_rows, table_bf), "ctx", -distance)
        query_span = span_id + distance
        if section == 0:
            terms = near_terms(
                far_q, far_g, k_rows, v_rows, query_span, length, band_width, relative_bucket_bias
            )
        else:
            chosen = far_table[:, section - 1].astype(jnp.int32)
            terms = far_terms(
                far_q,
                far_g,
                k_rows,
                v_rows,
                chosen,
                query_span,
                distance,
                length,
                relative_bucket_bias,
            )
        key_gradient = key_gradient + terms[1]
        value_gradient = value_gradient + terms[2]
        grad_bias = grad_bias + terms[3]
        back_q = from_behind(terms[0], "ctx", distance)
        grad_q = grad_q + back_q
    grad_bias = lax.psum(grad_bias, ("dp", "ctx"))
    return (
        grad_q[None].astype(jnp.bfloat16),
        key_gradient[None].astype(jnp.bfloat16),
        value_gradient[None].astype(jnp.bfloat16),
        grad_bias,
    )


def solution(mesh):
    in_specs = (
        P("dp", "ctx", None),
        P("dp", "ctx", None),
        P("dp", "ctx", None),
        P("dp", "ctx", None),
        P("dp", "ctx", None),
        P("dp", None),
        P("dp", None),
        P(),
    )
    out_specs = (P("dp", "ctx", None), P("dp", "ctx", None), P("dp", "ctx", None), P())
    return jax.shard_map(
        on_device, mesh=mesh, in_specs=in_specs, out_specs=out_specs, check_vma=False
    )
```

profile of v0, /device:TPU:12, one launch (start us, length us, event | category | flops | bytes accessed | tf_op | source)
XLA Modules:
  0.0 182.2 jit_solution(13746353603222092864)
XLA Ops:
  2.8 2.4 %collective-permute-start.3 = (bf16[2,2]{1,0:T(2,128)(2,1)S(1)}, bf16[2,2]{1,0:T(2,128)(2,1)S(1)}, u32[]{:S(2)}, u32[]{:S(2)}) collective-permute-start(bf16[2,2]{1,0:T(2,128)(2,1)S(1)} %convert_bitcast_fusion), channel_id=1, source_target_pairs={{2,0},{3,1},{4,2},{5,3},{6,4},{7,5},{10,8},{11,9},{12,10},{13,11},... | collective-permute-start | bytes 32 | tf_op jit(solution)/shard_map/ppermute | solution.py:16
  8.2 1.9 %collective-permute-start.4 = (bf16[256,512]{0,1:T(8,128)(2,1)}, bf16[256,512]{0,1:T(8,128)(2,1)}, u32[]{:S(2)}, u32[]{:S(2)}) collective-permute-start(bf16[256,512]{0,1:T(8,128)(2,1)} %bitcast.8), channel_id=1, source_target_pairs={{2,0},{3,1},{4,2},{5,3},{6,4},{7,5},{10,8},{11,9},{12,10},{13,11},... | collective-permute-start | bytes 786440 | tf_op jit(solution)/shard_map/ppermute | solution.py:16
  10.1 1.9 %collective-permute-start = (bf16[256,512]{0,1:T(8,128)(2,1)}, bf16[256,512]{0,1:T(8,128)(2,1)}, u32[]{:S(2)}, u32[]{:S(2)}) collective-permute-start(bf16[256,512]{0,1:T(8,128)(2,1)} %bitcast.8), channel_id=1, source_target_pairs={{1,0},{2,1},{3,2},{4,3},{5,4},{6,5},{7,6},{9,8},{10,9},{11,10},{12... | collective-permute-start | bytes 786440 | tf_op jit(solution)/shard_map/ppermute | solution.py:16
  18.4 2.3 %fusion.27 = f32[4,256,128]{1,2,0:T(8,128)} fusion(bf16[256,4,128]{0,2,1:T(8,128)(2,1)} %bitcast.83, f32[4,256,256]{2,1,0:T(8,128)S(1)} %fusion.3, pred[256,256]{1,0:T(8,128)(4,1)S(1)} %get-tuple-element.10), kind=kOutput, calls=%fused_computation.68 | convolution fusion | flops 68943872 | bytes 1900544 | tf_op jit(solution)/shard_map/ghqk,gqhd->gkhd/dot_general | solution.py:43
  26.1 2.1 %add.436 = f32[4,256,256]{2,1,0:T(8,128)S(1)} reshape(f32[4,2,128,2,128]{4,3,2,1,0:T(2,128)} %add.435) | data formatting | bytes 2097152 | tf_op jit(solution)/shard_map/add | solution.py:37
  28.2 2.1 %convolution_multiply_fusion.11 = f32[4,256,128]{1,2,0:T(8,128)} fusion(bf16[256,4,128]{0,2,1:T(8,128)(2,1)} %copy.171, f32[4,256,256]{2,1,0:T(8,128)S(1)} %fusion.5), kind=kOutput, calls=%fused_computation.40 | convolution fusion | flops 67502080 | bytes 1835008 | tf_op jit(solution)/shard_map/ghqk,gkhd->gqhd/dot_general | solution.py:54
  30.3 2.0 %copy.181 = f32[256,512]{1,0:T(8,128)} copy(f32[256,512]{0,1:T(8,128)} %bitcast.209) | data formatting | bytes 1048576 | tf_op jit(solution)/shard_map/squeeze;reshape | solution.py:118
  34.8 1.9 %collective-permute-start.5 = (bf16[256,512]{0,1:T(8,128)(2,1)S(1)}, bf16[256,512]{0,1:T(8,128)(2,1)}, u32[]{:S(2)}, u32[]{:S(2)}) collective-permute-start(bf16[256,512]{0,1:T(8,128)(2,1)S(1)} %bitcast.194), channel_id=1, source_target_pairs={{2,0},{3,1},{4,2},{5,3},{6,4},{7,5},{10,8},{11,9},{12,10},{13,11},... | collective-permute-start | bytes 786440 | tf_op jit(solution)/shard_map/ppermute | solution.py:16
  43.8 11.9 %collective-permute-done.5 = bf16[256,512]{0,1:T(8,128)(2,1)} collective-permute-done((bf16[256,512]{0,1:T(8,128)(2,1)S(1)}, bf16[256,512]{0,1:T(8,128)(2,1)}, u32[]{:S(2)}, u32[]{:S(2)}) %collective-permute-start.5) | collective-permute-done | bytes 262176 | tf_op jit(solution)/shard_map/ppermute | solution.py:16
  55.7 2.1 %collective-permute-start.1 = (bf16[256,512]{0,1:T(8,128)(2,1)S(1)}, bf16[256,512]{0,1:T(8,128)(2,1)S(1)}, u32[]{:S(2)}, u32[]{:S(2)}) collective-permute-start(bf16[256,512]{0,1:T(8,128)(2,1)S(1)} %bitcast.195), channel_id=1, source_target_pairs={{1,0},{2,1},{3,2},{4,3},{5,4},{6,5},{7,6},{9,8},{10,9},{11,10},{12... | collective-permute-start | bytes 786440 | tf_op jit(solution)/shard_map/ppermute | solution.py:16
  61.4 2.1 %fusion.107 = (f32[2,4]{1,0:T(2,128)}, bf16[2,4,128,128]{2,3,1,0:T(8,128)(2,1)S(1)}) fusion(f32[2,4,128,128]{2,3,1,0:T(8,128)S(1)} %fusion.19, bf16[2,128,4,128]{1,3,2,0:T(8,128)(2,1)} %bitcast.221, bf16[2,128,4,128]{1,0,3,2:T(2,128)(2,1)} %reshape.840, pred[2,128,128]{1,2,0:T(8,128)(4,1)S(1)} %and_and_fusion.1), kind=kOutput, calls=%fused_computation.191 | convolution fusion | flops 35127288 | bytes 1343520 | tf_op jit(solution)/shard_map/gqhd,gkhd->ghqk/dot_general | solution.py:46
  70.3 2.2 %fusion.108 = (f32[2,4]{1,0:T(2,128)}, bf16[2,4,128,128]{2,3,1,0:T(8,128)(2,1)S(1)}) fusion(f32[2,4,128,128]{2,3,1,0:T(8,128)} %fusion.16, bf16[2,128,4,128]{1,3,2,0:T(8,128)(2,1)S(1)} %bitcast.220, bf16[2,128,4,128]{1,0,3,2:T(2,128)(2,1)} %reshape.842, pred[2,128,128]{1,2,0:T(8,128)(4,1)S(1)} %and_and_fusion), kind=kOutput, calls=%fused_computation.192 | convolution fusion | flops 35127288 | bytes 1343520 | tf_op jit(solution)/shard_map/gqhd,gkhd->ghqk/dot_general | solution.py:46
  82.8 2.0 %copy.191 = f32[2,128,4,128]{3,2,1,0:T(4,128)} copy(f32[2,128,4,128]{1,3,2,0:T(8,128)} %fusion.17) | data formatting | bytes 1048576 | tf_op jit(solution)/shard_map/mul | solution.py:54
  86.7 2.0 %copy.206 = f32[2,128,4,128]{1,3,2,0:T(8,128)} copy(f32[2,128,4,128]{3,1,2,0:T(8,128)} %fusion.13) | data formatting | bytes 1048576 | tf_op jit(solution)/shard_map/mul | solution.py:58
  88.8 2.0 %copy.207 = f32[2,128,512]{2,0,1:T(2,128)} copy(f32[2,128,512]{1,2,0:T(8,128)} %bitcast.211) | data formatting | bytes 1048576 | tf_op jit(solution)/shard_map/reshape | solution.py:63
  90.8 2.1 %fusion.73 = f32[2,128,512]{2,0,1:T(2,128)S(1)} fusion(f32[2,128,512]{2,0,1:T(2,128)} %copy.207, s32[2]{0:T(128)S(1)} %get-tuple-element.6), kind=kOutput, calls=%fused_computation.131 | convolution fusion | flops 3145732 | bytes 1048584 | tf_op jit(solution)/shard_map/as,apc->spc/dot_general | solution.py:151
  93.8 2.0 %copy.224 = f32[2,128,512]{2,0,1:T(2,128)} copy(f32[2,128,512]{1,2,0:T(8,128)} %bitcast.217) | data formatting | bytes 1048576 | tf_op jit(solution)/shard_map/reshape | solution.py:64
  95.9 2.1 %fusion.67 = f32[2,128,512]{2,0,1:T(2,128)S(1)} fusion(f32[2,128,512]{2,0,1:T(2,128)} %copy.224, s32[2]{0:T(128)S(1)} %get-tuple-element.8), kind=kOutput, calls=%fused_computation.125 | convolution fusion | flops 3145732 | bytes 1048584 | tf_op jit(solution)/shard_map/as,apc->spc/dot_general | solution.py:154
  98.9 2.0 %copy.201 = f32[2,128,4,128]{3,2,1,0:T(4,128)} copy(f32[2,128,4,128]{1,3,2,0:T(8,128)} %fusion.14) | data formatting | bytes 1048576 | tf_op jit(solution)/shard_map/mul | solution.py:54
  100.9 1.9 %copy.292 = f32[32,8,4,128]{3,1,2,0:T(8,128)} copy(f32[32,8,4,128]{3,2,1,0:T(4,128)} %bitcast.212) | data formatting | bytes 1048576
  102.8 2.0 %copy.213 = f32[2,128,4,128]{1,3,2,0:T(8,128)} copy(f32[2,128,4,128]{3,1,2,0:T(8,128)} %fusion.12) | data formatting | bytes 1048576 | tf_op jit(solution)/shard_map/mul | solution.py:58
  104.8 2.0 %copy.214 = f32[2,128,512]{2,0,1:T(2,128)} copy(f32[2,128,512]{1,2,0:T(8,128)} %bitcast.213) | data formatting | bytes 1048576 | tf_op jit(solution)/shard_map/reshape | solution.py:63
  106.9 2.2 %fusion.69 = f32[2,128,512]{2,0,1:T(2,128)S(1)} fusion(f32[2,128,512]{2,0,1:T(2,128)} %copy.214, s32[2]{0:T(128)S(1)} %get-tuple-element.8), kind=kOutput, calls=%fused_computation.127 | convolution fusion | flops 3145732 | bytes 1048584 | tf_op jit(solution)/shard_map/as,apc->spc/dot_general | solution.py:151
  110.0 3.1 %collective-permute-start.10 = (f32[256,512]{1,0:T(8,128)}, f32[256,512]{1,0:T(8,128)}, u32[]{:S(2)}, u32[]{:S(2)}) collective-permute-start(f32[256,512]{1,0:T(8,128)} %bitcast.181), channel_id=1, source_target_pairs={{0,4},{1,5},{2,6},{3,7},{8,12},{9,13},{10,14},{11,15},{16,20},{17,... | collective-permute-start | bytes 1572872 | tf_op jit(solution)/shard_map/ppermute | solution.py:16
  113.1 2.1 %collective-permute-start.6 = (f32[256,512]{1,0:T(8,128)}, f32[256,512]{1,0:T(8,128)}, u32[]{:S(2)}, u32[]{:S(2)}) collective-permute-start(f32[256,512]{1,0:T(8,128)} %bitcast.182), channel_id=1, source_target_pairs={{0,2},{1,3},{2,4},{3,5},{4,6},{5,7},{8,10},{9,11},{10,12},{11,13},... | collective-permute-start | bytes 1572872 | tf_op jit(solution)/shard_map/ppermute | solution.py:16
  115.2 2.2 %convolution_add_fusion = f32[4,256,128]{1,2,0:T(8,128)} fusion(f32[4,256,128]{1,2,0:T(8,128)S(1)} %copy-done.35, bf16[256,4,128]{0,2,1:T(8,128)(2,1)} %bitcast.9, f32[4,256,256]{2,1,0:T(8,128)S(1)} %copy-done.15, pred[256,256]{1,0:T(8,128)(4,1)S(1)} %get-tuple-element.9), kind=kOutput, calls=%fused_computation.36 | convolution fusion | flops 69074944 | bytes 2424832 | tf_op jit(solution)/shard_map/ghqk,gqhd->gkhd/dot_general | solution.py:43
  117.4 2.0 %copy.221 = f32[1,256,512]{2,1,0:T(8,128)} copy(f32[1,256,512]{1,2,0:T(8,128)} %bitcast.219) | data formatting | bytes 1048576 | tf_op jit(solution)/shard_map/add | solution.py:199
  119.5 2.1 %fusion.20 = f32[4,256,128]{1,2,0:T(8,128)} fusion(f32[4,256,128]{1,2,0:T(8,128)} %fusion.33, bf16[256,4,128]{0,2,1:T(8,128)(2,1)S(1)} %bitcast.216, f32[4,256,256]{2,1,0:T(8,128)S(1)} %fusion.2), kind=kOutput, calls=%fused_computation.38 | convolution fusion | flops 67633152 | bytes 2359296 | tf_op jit(solution)/shard_map/ghqk,gqhd->gkhd/dot_general | solution.py:58
  127.2 42.2 %psum.7 = f32[4,7]{1,0:T(4,128)} all-reduce(f32[4,7]{1,0:T(4,128)S(1)} %convolution_add_fusion.2), channel_id=1, replica_groups=mesh['dp'=4,'ctx'=8] {'dp','ctx'}, use_global_device_ids=true, to_apply=%region_4.6 | all-reduce | flops 28 | bytes 224 | tf_op jit(solution)/shard_map/psum | solution.py:203
  169.4 1.9 %collective-permute-start.2 = (f32[256,512]{1,0:T(8,128)}, f32[256,512]{1,0:T(8,128)S(1)}, u32[]{:S(2)}, u32[]{:S(2)}) collective-permute-start(f32[256,512]{1,0:T(8,128)} %copy.180), channel_id=1, source_target_pairs={{0,1},{1,2},{2,3},{3,4},{4,5},{5,6},{6,7},{8,9},{9,10},{10,11},{11... | collective-permute-start | bytes 1572872 | tf_op jit(solution)/shard_map/ppermute | solution.py:16
  173.5 6.6 %collective-permute-done.2 = f32[256,512]{1,0:T(8,128)S(1)} collective-permute-done((f32[256,512]{1,0:T(8,128)}, f32[256,512]{1,0:T(8,128)S(1)}, u32[]{:S(2)}, u32[]{:S(2)}) %collective-permute-start.2) | collective-permute-done | bytes 524320 | tf_op jit(solution)/shard_map/ppermute | solution.py:16
  180.1 2.1 %fusion.30 = bf16[1,256,512]{2,1,0:T(8,128)(2,1)} fusion(f32[256,512]{1,0:T(8,128)} %collective-permute-done.10, f32[256,512]{1,0:T(8,128)} %collective-permute-done.6, f32[256,512]{1,0:T(8,128)S(1)} %copy-done.13, f32[256,512]{1,0:T(8,128)S(1)} %collective-permute-done.2), kind=kLoop, calls=%fused_computation.71 | loop fusion | flops 524288 | bytes 2359296 | tf_op jit(solution)/shard_map/convert_element_type | solution.py:205
  (167 shorter events, 57.8 us)
Async XLA Ops:
  0.6 12.8 %copy-start = (f32[4,7]{1,0:T(4,128)S(1)}, f32[4,7]{1,0:T(4,128)}, u32[]{:S(2)}) copy-start(f32[4,7]{1,0:T(4,128)} %param.17) | copy-start | bytes 340
  1.3 12.4 %copy-start.7 = (bf16[1,256,512]{2,1,0:T(8,128)(2,1)S(1)}, bf16[1,256,512]{2,1,0:T(8,128)(2,1)}, u32[]{:S(2)}) copy-start(bf16[1,256,512]{2,1,0:T(8,128)(2,1)} %param.11) | copy-start | bytes 786436
  1.3 31.4 %collective-permute-start.7 = (bf16[2,2]{1,0:T(2,128)(2,1)S(1)}, bf16[2,2]{1,0:T(2,128)(2,1)S(1)}, u32[]{:S(2)}, u32[]{:S(2)}) collective-permute-start(bf16[2,2]{1,0:T(2,128)(2,1)S(1)} %convert_bitcast_fusion), channel_id=1, source_target_pairs={{4,0},{5,1},{6,2},{7,3},{12,8},{13,9},{14,10},{15,11},{20,16},{21,... | collective-permute-start | bytes 32 | tf_op jit(solution)/shard_map/ppermute | solution.py:16
  2.8 32.0 %collective-permute-start.3 = (bf16[2,2]{1,0:T(2,128)(2,1)S(1)}, bf16[2,2]{1,0:T(2,128)(2,1)S(1)}, u32[]{:S(2)}, u32[]{:S(2)}) collective-permute-start(bf16[2,2]{1,0:T(2,128)(2,1)S(1)} %convert_bitcast_fusion), channel_id=1, source_target_pairs={{2,0},{3,1},{4,2},{5,3},{6,4},{7,5},{10,8},{11,9},{12,10},{13,11},... | collective-permute-start | bytes 32 | tf_op jit(solution)/shard_map/ppermute | solution.py:16
  6.9 61.6 %collective-permute-start.8 = (bf16[256,512]{0,1:T(8,128)(2,1)}, bf16[256,512]{0,1:T(8,128)(2,1)}, u32[]{:S(2)}, u32[]{:S(2)}) collective-permute-start(bf16[256,512]{0,1:T(8,128)(2,1)} %bitcast.8), channel_id=1, source_target_pairs={{4,0},{5,1},{6,2},{7,3},{12,8},{13,9},{14,10},{15,11},{20,16},{21,... | collective-permute-start | bytes 786440 | tf_op jit(solution)/shard_map/ppermute | solution.py:16
  8.2 51.5 %collective-permute-start.4 = (bf16[256,512]{0,1:T(8,128)(2,1)}, bf16[256,512]{0,1:T(8,128)(2,1)}, u32[]{:S(2)}, u32[]{:S(2)}) collective-permute-start(bf16[256,512]{0,1:T(8,128)(2,1)} %bitcast.8), channel_id=1, source_target_pairs={{2,0},{3,1},{4,2},{5,3},{6,4},{7,5},{10,8},{11,9},{12,10},{13,11},... | collective-permute-start | bytes 786440 | tf_op jit(solution)/shard_map/ppermute | solution.py:16
  10.1 67.7 %collective-permute-start = (bf16[256,512]{0,1:T(8,128)(2,1)}, bf16[256,512]{0,1:T(8,128)(2,1)}, u32[]{:S(2)}, u32[]{:S(2)}) collective-permute-start(bf16[256,512]{0,1:T(8,128)(2,1)} %bitcast.8), channel_id=1, source_target_pairs={{1,0},{2,1},{3,2},{4,3},{5,4},{6,5},{7,6},{9,8},{10,9},{11,10},{12... | collective-permute-start | bytes 786440 | tf_op jit(solution)/shard_map/ppermute | solution.py:16
  12.1 1.3 copy-start.31
  15.7 2.0 %copy-start.2 = (bf16[1,256,512]{1,2,0:T(8,128)(2,1)}, bf16[1,256,512]{1,2,0:T(8,128)(2,1)S(1)}, u32[]{:S(2)}) copy-start(bf16[1,256,512]{1,2,0:T(8,128)(2,1)S(1)} %copy.255) | copy-start | bytes 786436
  18.4 2.3 %copy-start.18 = (bf16[256,4,128]{2,1,0:T(4,128)(2,1)S(1)}, bf16[256,4,128]{2,1,0:T(4,128)(2,1)}, u32[]{:S(2)}) copy-start(bf16[256,4,128]{2,1,0:T(4,128)(2,1)} %reshape.770) | copy-start | bytes 786436
  20.6 1.6 copy-start.3
  32.3 4.6 %copy-start.6 = (bf16[1,256,512]{2,1,0:T(8,128)(2,1)S(1)}, bf16[1,256,512]{2,1,0:T(8,128)(2,1)}, u32[]{:S(2)}) copy-start(bf16[1,256,512]{2,1,0:T(8,128)(2,1)} %param.12) | copy-start | bytes 786436
  33.3 32.4 %collective-permute-start.9 = (bf16[256,512]{0,1:T(8,128)(2,1)S(1)}, bf16[256,512]{0,1:T(8,128)(2,1)}, u32[]{:S(2)}, u32[]{:S(2)}) collective-permute-start(bf16[256,512]{0,1:T(8,128)(2,1)S(1)} %bitcast.193), channel_id=1, source_target_pairs={{4,0},{5,1},{6,2},{7,3},{12,8},{13,9},{14,10},{15,11},{20,16},{21,... | collective-permute-start | bytes 786440 | tf_op jit(solution)/shard_map/ppermute | solution.py:16
  34.8 5.5 %copy-start.27 = (s32[2]{0:T(128)}, s32[2]{0:T(128)S(1)}, u32[]{:S(2)}) copy-start(s32[2]{0:T(128)S(1)} %get-tuple-element.15) | copy-start | bytes 28
  34.8 20.9 %collective-permute-start.5 = (bf16[256,512]{0,1:T(8,128)(2,1)S(1)}, bf16[256,512]{0,1:T(8,128)(2,1)}, u32[]{:S(2)}, u32[]{:S(2)}) collective-permute-start(bf16[256,512]{0,1:T(8,128)(2,1)S(1)} %bitcast.194), channel_id=1, source_target_pairs={{2,0},{3,1},{4,2},{5,3},{6,4},{7,5},{10,8},{11,9},{12,10},{13,11},... | collective-permute-start | bytes 786440 | tf_op jit(solution)/shard_map/ppermute | solution.py:16
  36.9 4.1 %copy-start.29 = (s32[2]{0:T(128)}, s32[2]{0:T(128)S(1)}, u32[]{:S(2)}) copy-start(s32[2]{0:T(128)S(1)} %get-tuple-element.11) | copy-start | bytes 28
  55.7 19.0 %collective-permute-start.1 = (bf16[256,512]{0,1:T(8,128)(2,1)S(1)}, bf16[256,512]{0,1:T(8,128)(2,1)S(1)}, u32[]{:S(2)}, u32[]{:S(2)}) collective-permute-start(bf16[256,512]{0,1:T(8,128)(2,1)S(1)} %bitcast.195), channel_id=1, source_target_pairs={{1,0},{2,1},{3,2},{4,3},{5,4},{6,5},{7,6},{9,8},{10,9},{11,10},{12... | collective-permute-start | bytes 786440 | tf_op jit(solution)/shard_map/ppermute | solution.py:16
  68.5 1.8 copy-start.20
  75.0 2.8 %copy-start.14 = (f32[4,256,256]{2,1,0:T(8,128)}, f32[4,256,256]{2,1,0:T(8,128)S(1)}, u32[]{:S(2)}) copy-start(f32[4,256,256]{2,1,0:T(8,128)S(1)} %fusion) | copy-start | bytes 3145732
  75.0 1.4 copy-start.16
  75.0 1.7 copy-start.22
  76.7 1.2 copy-start.19
  77.9 1.6 copy-start.1
  106.9 8.3 %copy-start.15 = (f32[4,256,256]{2,1,0:T(8,128)S(1)}, f32[4,256,256]{2,1,0:T(8,128)}, u32[]{:S(2)}) copy-start(f32[4,256,256]{2,1,0:T(8,128)} %copy-done.14) | copy-start | bytes 3145732
  109.1 6.2 %copy-start.35 = (f32[4,256,128]{1,2,0:T(8,128)S(1)}, f32[4,256,128]{1,2,0:T(8,128)}, u32[]{:S(2)}) copy-start(f32[4,256,128]{1,2,0:T(8,128)} %fusion.27) | copy-start | bytes 1572868
  110.0 63.5 %collective-permute-start.10 = (f32[256,512]{1,0:T(8,128)}, f32[256,512]{1,0:T(8,128)}, u32[]{:S(2)}, u32[]{:S(2)}) collective-permute-start(f32[256,512]{1,0:T(8,128)} %bitcast.181), channel_id=1, source_target_pairs={{0,4},{1,5},{2,6},{3,7},{8,12},{9,13},{10,14},{11,15},{16,20},{17,... | collective-permute-start | bytes 1572872 | tf_op jit(solution)/shard_map/ppermute | solution.py:16
  113.1 60.4 %collective-permute-start.6 = (f32[256,512]{1,0:T(8,128)}, f32[256,512]{1,0:T(8,128)}, u32[]{:S(2)}, u32[]{:S(2)}) collective-permute-start(f32[256,512]{1,0:T(8,128)} %bitcast.182), channel_id=1, source_target_pairs={{0,2},{1,3},{2,4},{3,5},{4,6},{5,7},{8,10},{9,11},{10,12},{11,13},... | collective-permute-start | bytes 1572872 | tf_op jit(solution)/shard_map/ppermute | solution.py:16
  126.1 45.2 %copy-start.10 = (f32[2,128,512]{2,1,0:T(8,128)S(1)}, f32[2,128,512]{2,1,0:T(8,128)}, u32[]{:S(2)}) copy-start(f32[2,128,512]{2,1,0:T(8,128)} %copy.225) | copy-start | bytes 1572868
  126.1 45.2 %copy-start.12 = (f32[1,256,512]{2,1,0:T(8,128)S(1)}, f32[1,256,512]{2,1,0:T(8,128)}, u32[]{:S(2)}) copy-start(f32[1,256,512]{2,1,0:T(8,128)} %copy.221) | copy-start | bytes 1572868
  169.4 10.7 %collective-permute-start.2 = (f32[256,512]{1,0:T(8,128)}, f32[256,512]{1,0:T(8,128)S(1)}, u32[]{:S(2)}, u32[]{:S(2)}) collective-permute-start(f32[256,512]{1,0:T(8,128)} %copy.180), channel_id=1, source_target_pairs={{0,1},{1,2},{2,3},{3,4},{4,5},{5,6},{6,7},{8,9},{9,10},{10,11},{11... | collective-permute-start | bytes 1572872 | tf_op jit(solution)/shard_map/ppermute | solution.py:16
  171.3 1.3 copy-start.11
  172.6 7.5 %copy-start.13 = (f32[256,512]{1,0:T(8,128)S(1)}, f32[256,512]{1,0:T(8,128)}, u32[]{:S(2)}) copy-start(f32[256,512]{1,0:T(8,128)} %copy.181) | copy-start | bytes 1572868
  (15 other events, 12.0 us)
where the time goes:
time: 184 us; the launch traced here: 182 us
  local copies, waits for them, and re-layouts  54.7 us (30%)
  blocking collectives  42.2 us (23%)
  matrix products  36.1 us (20%)
  starting transfers between devices  21.3 us (12%)
  waiting for transfers between devices  18.6 us (10%)
  other arithmetic  6.7 us (4%)
  between operations  2.64 us (1%)
    psum x1, blocking collectives, on_device(): grad_bias = lax.psum(grad_bias, ('dp', 'ctx'))  42.2 us
    ppermute x11, starting transfers between devices, from_behind(): return lax.ppermute(array, axis, pairs)  21.3 us
    ppermute x11, waiting for transfers between devices, from_behind(): return lax.ppermute(array, axis, pairs)  18.6 us
    unnamed x74, local copies, waits for them, and re-layouts  10.7 us
    dot_general x4, matrix products, tile_grads(): jnp.einsum('gqhd,gkhd->ghqk', g_heads, v_heads, preferred_element_type=jn...  7.51 us
    dot_general x4, matrix products, tile_grads(): jnp.einsum('ghqk,gqhd->gkhd', weights_bf, g_heads, preferred_element_type...  6.73 us
    dot_general x4, matrix products, tile_grads(): jnp.einsum('ghqk,gqhd->gkhd', dscore_bf, q_heads, preferred_element_type=...  5.31 us
    add x4, local copies, waits for them, and re-layouts, tile_grads(): score + bias_tile[:, :, :, None, :, None]  4.55 us
  transfers between devices with their start and end apart: 11, of which 2 were waited for; matrix products, arithmetic and copies ran while one was open for 31% of the time, Pallas kernels for 0%

commit v1 on v0

--- a/solution.py
+++ b/solution.py
@@ -200,7 +200,7 @@
         grad_bias = grad_bias + terms[3]
         back_q = from_behind(terms[0], "ctx", distance)
         grad_q = grad_q + back_q
-    grad_bias = lax.psum(grad_bias, ("dp", "ctx"))
+    grad_bias = lax.psum(lax.psum(grad_bias, "ctx"), "dp")
     return (
         grad_q[None].astype(jnp.bfloat16),
         key_gradient[None].astype(jnp.bfloat16),

time: 184 us -> 173 us (0.940); the launches traced: 182 us -> 169 us
  blocking collectives: 42.2 us -> 33 us
  matrix products: 36.1 us -> 34.2 us
    psum x1 -> x2, blocking collectives: 42.2 us -> 33 us  [on_device(): grad_bias = lax.psum(lax.psum(grad_bias, 'ctx'), 'dp')]
    unnamed x74 -> x80, local copies, waits for them, and re-layouts: 10.7 us -> 10.4 us
  transfers between devices with their start and end apart: 11 -> 11, of which waited for: 2 -> 2; matrix products, arithmetic and copies ran while one was open for 31% -> 33% of each run, Pallas kernels for 0% -> 0%
where the time goes in v1:
time: 173 us; the launch traced here: 169 us
  local copies, waits for them, and re-layouts  52.9 us (31%)
  matrix products  34.2 us (20%)
  blocking collectives  33 us (19%)
  starting transfers between devices  21.1 us (12%)
  waiting for transfers between devices  18.5 us (11%)
  other arithmetic  6.7 us (4%)
  between operations  2.66 us (2%)
    psum x2, blocking collectives, on_device(): grad_bias = lax.psum(lax.psum(grad_bias, 'ctx'), 'dp')  33 us
    ppermute x11, starting transfers between devices, from_behind(): return lax.ppermute(array, axis, pairs)  21.1 us
    ppermute x11, waiting for transfers between devices, from_behind(): return lax.ppermute(array, axis, pairs)  18.5 us
    unnamed x80, local copies, waits for them, and re-layouts  10.4 us
    dot_general x4, matrix products, tile_grads(): jnp.einsum('gqhd,gkhd->ghqk', g_heads, v_heads, preferred_element_type=jn...  7.41 us
    dot_general x4, matrix products, tile_grads(): jnp.einsum('ghqk,gqhd->gkhd', weights_bf, g_heads, preferred_element_type...  6.73 us
    dot_general x4, matrix products, tile_grads(): jnp.einsum('ghqk,gkhd->gqhd', dscore_bf, k_heads, preferred_element_type=...  5.19 us
    add x4, local copies, waits for them, and re-layouts, tile_grads(): score + bias_tile[:, :, :, None, :, None]  4.55 us
  transfers between devices with their start and end apart: 11, of which 2 were waited for; matrix products, arithmetic and copies ran while one was open for 33% of the time, Pallas kernels for 0%

profile of v1, /device:TPU:12, one launch (start us, length us, event | category | flops | bytes accessed | tf_op | source)
XLA Modules:
  0.0 169.1 jit_solution(1535710874003048845)
XLA Ops:
  2.8 2.4 %collective-permute-start.3 = (bf16[2,2]{1,0:T(2,128)(2,1)S(1)}, bf16[2,2]{1,0:T(2,128)(2,1)S(1)}, u32[]{:S(2)}, u32[]{:S(2)}) collective-permute-start(bf16[2,2]{1,0:T(2,128)(2,1)S(1)} %convert_bitcast_fusion), channel_id=1, source_target_pairs={{2,0},{3,1},{4,2},{5,3},{6,4},{7,5},{10,8},{11,9},{12,10},{13,11},... | collective-permute-start | bytes 32 | tf_op jit(solution)/shard_map/ppermute | solution.py:16
  8.2 1.9 %collective-permute-start.4 = (bf16[256,512]{0,1:T(8,128)(2,1)}, bf16[256,512]{0,1:T(8,128)(2,1)}, u32[]{:S(2)}, u32[]{:S(2)}) collective-permute-start(bf16[256,512]{0,1:T(8,128)(2,1)} %bitcast.8), channel_id=1, source_target_pairs={{2,0},{3,1},{4,2},{5,3},{6,4},{7,5},{10,8},{11,9},{12,10},{13,11},... | collective-permute-start | bytes 786440 | tf_op jit(solution)/shard_map/ppermute | solution.py:16
  10.1 1.9 %collective-permute-start = (bf16[256,512]{0,1:T(8,128)(2,1)}, bf16[256,512]{0,1:T(8,128)(2,1)}, u32[]{:S(2)}, u32[]{:S(2)}) collective-permute-start(bf16[256,512]{0,1:T(8,128)(2,1)} %bitcast.8), channel_id=1, source_target_pairs={{1,0},{2,1},{3,2},{4,3},{5,4},{6,5},{7,6},{9,8},{10,9},{11,10},{12... | collective-permute-start | bytes 786440 | tf_op jit(solution)/shard_map/ppermute | solution.py:16
  18.4 2.3 %fusion.27 = f32[4,256,128]{1,2,0:T(8,128)} fusion(bf16[256,4,128]{0,2,1:T(8,128)(2,1)} %bitcast.83, f32[4,256,256]{2,1,0:T(8,128)S(1)} %fusion.3, pred[256,256]{1,0:T(8,128)(4,1)S(1)} %get-tuple-element.10), kind=kOutput, calls=%fused_computation.68 | convolution fusion | flops 68943872 | bytes 1900544 | tf_op jit(solution)/shard_map/ghqk,gqhd->gkhd/dot_general | solution.py:43
  26.1 2.1 %add.438 = f32[4,256,256]{2,1,0:T(8,128)S(1)} reshape(f32[4,2,128,2,128]{4,3,2,1,0:T(2,128)} %add.437) | data formatting | bytes 2097152 | tf_op jit(solution)/shard_map/add | solution.py:37
  28.2 2.1 %convolution_multiply_fusion.11 = f32[4,256,128]{1,2,0:T(8,128)} fusion(bf16[256,4,128]{0,2,1:T(8,128)(2,1)} %copy.171, f32[4,256,256]{2,1,0:T(8,128)S(1)} %fusion.5), kind=kOutput, calls=%fused_computation.40 | convolution fusion | flops 67502080 | bytes 1835008 | tf_op jit(solution)/shard_map/ghqk,gkhd->gqhd/dot_general | solution.py:54
  30.3 2.0 %copy.181 = f32[256,512]{1,0:T(8,128)} copy(f32[256,512]{0,1:T(8,128)} %bitcast.209) | data formatting | bytes 1048576 | tf_op jit(solution)/shard_map/squeeze;reshape | solution.py:118
  34.8 1.9 %collective-permute-start.5 = (bf16[256,512]{0,1:T(8,128)(2,1)S(1)}, bf16[256,512]{0,1:T(8,128)(2,1)}, u32[]{:S(2)}, u32[]{:S(2)}) collective-permute-start(bf16[256,512]{0,1:T(8,128)(2,1)S(1)} %bitcast.194), channel_id=1, source_target_pairs={{2,0},{3,1},{4,2},{5,3},{6,4},{7,5},{10,8},{11,9},{12,10},{13,11},... | collective-permute-start | bytes 786440 | tf_op jit(solution)/shard_map/ppermute | solution.py:16
  43.8 11.8 %collective-permute-done.5 = bf16[256,512]{0,1:T(8,128)(2,1)} collective-permute-done((bf16[256,512]{0,1:T(8,128)(2,1)S(1)}, bf16[256,512]{0,1:T(8,128)(2,1)}, u32[]{:S(2)}, u32[]{:S(2)}) %collective-permute-start.5) | collective-permute-done | bytes 262176 | tf_op jit(solution)/shard_map/ppermute | solution.py:16
  55.6 2.1 %collective-permute-start.1 = (bf16[256,512]{0,1:T(8,128)(2,1)S(1)}, bf16[256,512]{0,1:T(8,128)(2,1)S(1)}, u32[]{:S(2)}, u32[]{:S(2)}) collective-permute-start(bf16[256,512]{0,1:T(8,128)(2,1)S(1)} %bitcast.195), channel_id=1, source_target_pairs={{1,0},{2,1},{3,2},{4,3},{5,4},{6,5},{7,6},{9,8},{10,9},{11,10},{12... | collective-permute-start | bytes 786440 | tf_op jit(solution)/shard_map/ppermute | solution.py:16
  59.7 1.9 %reshape.840 = bf16[2,128,4,128]{1,0,3,2:T(2,128)(2,1)} reshape(bf16[256,512]{0,1:T(8,128)(2,1)} %collective-permute-done.4) | data formatting | bytes 524288 | tf_op jit(solution)/shard_map/reshape;reshape | solution.py:28
  61.7 2.1 %fusion.107 = (f32[2,4]{1,0:T(2,128)}, bf16[2,4,128,128]{2,3,1,0:T(8,128)(2,1)S(1)}) fusion(f32[2,4,128,128]{2,3,1,0:T(8,128)S(1)} %fusion.19, bf16[2,128,4,128]{1,3,2,0:T(8,128)(2,1)} %bitcast.221, bf16[2,128,4,128]{1,0,3,2:T(2,128)(2,1)} %reshape.840, pred[2,128,128]{1,2,0:T(8,128)(4,1)S(1)} %and_and_fusion.1), kind=kOutput, calls=%fused_computation.191 | convolution fusion | flops 35127288 | bytes 1343520 | tf_op jit(solution)/shard_map/gqhd,gkhd->ghqk/dot_general | solution.py:46
  67.1 1.9 %reshape.842 = bf16[2,128,4,128]{1,0,3,2:T(2,128)(2,1)} reshape(bf16[256,512]{0,1:T(8,128)(2,1)} %collective-permute-done.8) | data formatting | bytes 524288 | tf_op jit(solution)/shard_map/reshape;reshape | solution.py:28
  69.0 2.1 %fusion.108 = (f32[2,4]{1,0:T(2,128)}, bf16[2,4,128,128]{2,3,1,0:T(8,128)(2,1)S(1)}) fusion(f32[2,4,128,128]{2,3,1,0:T(8,128)S(1)} %fusion.16, bf16[2,128,4,128]{1,3,2,0:T(8,128)(2,1)} %bitcast.220, bf16[2,128,4,128]{1,0,3,2:T(2,128)(2,1)} %reshape.842, pred[2,128,128]{1,2,0:T(8,128)(4,1)S(1)} %and_and_fusion), kind=kOutput, calls=%fused_computation.192 | convolution fusion | flops 35127288 | bytes 1343520 | tf_op jit(solution)/shard_map/gqhd,gkhd->ghqk/dot_general | solution.py:46
  82.3 2.0 %copy.191 = f32[2,128,4,128]{3,2,1,0:T(4,128)} copy(f32[2,128,4,128]{1,3,2,0:T(8,128)} %fusion.17) | data formatting | bytes 1048576 | tf_op jit(solution)/shard_map/mul | solution.py:54
  89.7 2.0 %copy.224 = f32[2,128,512]{2,0,1:T(2,128)} copy(f32[2,128,512]{1,2,0:T(8,128)} %bitcast.217) | data formatting | bytes 1048576 | tf_op jit(solution)/shard_map/reshape | solution.py:64
  91.7 2.1 %fusion.67 = f32[2,128,512]{2,0,1:T(2,128)S(1)} fusion(f32[2,128,512]{2,0,1:T(2,128)} %copy.224, s32[2]{0:T(128)S(1)} %get-tuple-element.8), kind=kOutput, calls=%fused_computation.125 | convolution fusion | flops 3145732 | bytes 1048584 | tf_op jit(solution)/shard_map/as,apc->spc/dot_general | solution.py:154
  94.7 2.0 %copy.201 = f32[2,128,4,128]{3,2,1,0:T(4,128)} copy(f32[2,128,4,128]{1,3,2,0:T(8,128)} %fusion.14) | data formatting | bytes 1048576 | tf_op jit(solution)/shard_map/mul | solution.py:54
  98.6 2.0 %copy.213 = f32[2,128,4,128]{1,3,2,0:T(8,128)} copy(f32[2,128,4,128]{3,1,2,0:T(8,128)} %fusion.12) | data formatting | bytes 1048576 | tf_op jit(solution)/shard_map/mul | solution.py:58
  100.7 2.1 %copy.214 = f32[2,128,512]{2,0,1:T(2,128)} copy(f32[2,128,512]{1,2,0:T(8,128)} %bitcast.213) | data formatting | bytes 1048576 | tf_op jit(solution)/shard_map/reshape | solution.py:63
  102.7 2.2 %fusion.69 = f32[2,128,512]{2,0,1:T(2,128)S(1)} fusion(f32[2,128,512]{2,0,1:T(2,128)} %copy.214, s32[2]{0:T(128)S(1)} %get-tuple-element.8), kind=kOutput, calls=%fused_computation.127 | convolution fusion | flops 3145732 | bytes 1048584 | tf_op jit(solution)/shard_map/as,apc->spc/dot_general | solution.py:151
  105.8 3.1 %collective-permute-start.10 = (f32[256,512]{1,0:T(8,128)}, f32[256,512]{1,0:T(8,128)}, u32[]{:S(2)}, u32[]{:S(2)}) collective-permute-start(f32[256,512]{1,0:T(8,128)} %bitcast.181), channel_id=1, source_target_pairs={{0,4},{1,5},{2,6},{3,7},{8,12},{9,13},{10,14},{11,15},{16,20},{17,... | collective-permute-start | bytes 1572872 | tf_op jit(solution)/shard_map/ppermute | solution.py:16
  108.9 1.9 %collective-permute-start.6 = (f32[256,512]{1,0:T(8,128)}, f32[256,512]{1,0:T(8,128)}, u32[]{:S(2)}, u32[]{:S(2)}) collective-permute-start(f32[256,512]{1,0:T(8,128)} %bitcast.182), channel_id=1, source_target_pairs={{0,2},{1,3},{2,4},{3,5},{4,6},{5,7},{8,10},{9,11},{10,12},{11,13},... | collective-permute-start | bytes 1572872 | tf_op jit(solution)/shard_map/ppermute | solution.py:16
  110.9 2.2 %convolution_add_fusion = f32[4,256,128]{1,2,0:T(8,128)} fusion(f32[4,256,128]{1,2,0:T(8,128)S(1)} %copy-done.38, bf16[256,4,128]{0,2,1:T(8,128)(2,1)} %bitcast.9, f32[4,256,256]{2,1,0:T(8,128)S(1)} %copy-done.16, pred[256,256]{1,0:T(8,128)(4,1)S(1)} %get-tuple-element.9), kind=kOutput, calls=%fused_computation.36 | convolution fusion | flops 69074944 | bytes 2424832 | tf_op jit(solution)/shard_map/ghqk,gqhd->gkhd/dot_general | solution.py:43
  113.1 2.0 %copy.221 = f32[1,256,512]{2,1,0:T(8,128)} copy(f32[1,256,512]{1,2,0:T(8,128)} %bitcast.219) | data formatting | bytes 1048576 | tf_op jit(solution)/shard_map/add | solution.py:199
  115.1 2.1 %fusion.20 = f32[4,256,128]{1,2,0:T(8,128)} fusion(f32[4,256,128]{1,2,0:T(8,128)} %fusion.33, bf16[256,4,128]{0,2,1:T(8,128)(2,1)S(1)} %bitcast.216, f32[4,256,256]{2,1,0:T(8,128)S(1)} %fusion.2), kind=kOutput, calls=%fused_computation.38 | convolution fusion | flops 67633152 | bytes 2359296 | tf_op jit(solution)/shard_map/ghqk,gqhd->gkhd/dot_general | solution.py:58
  117.2 2.0 %copy.209 = f32[1,256,512]{2,1,0:T(8,128)} copy(f32[1,256,512]{1,2,0:T(8,128)} %bitcast.214) | data formatting | bytes 1048576 | tf_op jit(solution)/shard_map/add | solution.py:198
  123.3 23.5 %psum.14 = f32[4,7]{1,0:T(4,128)S(1)} all-reduce(f32[4,7]{1,0:T(4,128)S(1)} %convolution_add_fusion.2), channel_id=1, replica_groups=mesh['dp'=4,'ctx'=8] {'ctx'}, use_global_device_ids=true, to_apply=%region_4.6 | all-reduce | flops 28 | bytes 224 | tf_op jit(solution)/shard_map/psum | solution.py:203
  146.7 9.5 %psum.15 = f32[4,7]{1,0:T(4,128)} all-reduce(f32[4,7]{1,0:T(4,128)S(1)} %psum.14), channel_id=1, replica_groups=mesh['dp'=4,'ctx'=8] {'dp'}, use_global_device_ids=true, to_apply=%region_5.7 | all-reduce | flops 28 | bytes 224 | tf_op jit(solution)/shard_map/psum | solution.py:203
  156.2 1.9 %collective-permute-start.2 = (f32[256,512]{1,0:T(8,128)}, f32[256,512]{1,0:T(8,128)S(1)}, u32[]{:S(2)}, u32[]{:S(2)}) collective-permute-start(f32[256,512]{1,0:T(8,128)} %copy.180), channel_id=1, source_target_pairs={{0,1},{1,2},{2,3},{3,4},{4,5},{5,6},{6,7},{8,9},{9,10},{10,11},{11... | collective-permute-start | bytes 1572872 | tf_op jit(solution)/shard_map/ppermute | solution.py:16
  160.3 6.6 %collective-permute-done.2 = f32[256,512]{1,0:T(8,128)S(1)} collective-permute-done((f32[256,512]{1,0:T(8,128)}, f32[256,512]{1,0:T(8,128)S(1)}, u32[]{:S(2)}, u32[]{:S(2)}) %collective-permute-start.2) | collective-permute-done | bytes 524320 | tf_op jit(solution)/shard_map/ppermute | solution.py:16
  166.9 2.1 %fusion.30 = bf16[1,256,512]{2,1,0:T(8,128)(2,1)} fusion(f32[256,512]{1,0:T(8,128)} %collective-permute-done.10, f32[256,512]{1,0:T(8,128)} %collective-permute-done.6, f32[256,512]{1,0:T(8,128)S(1)} %copy-done.14, f32[256,512]{1,0:T(8,128)S(1)} %collective-permute-done.2), kind=kLoop, calls=%fused_computation.71 | loop fusion | flops 524288 | bytes 2359296 | tf_op jit(solution)/shard_map/convert_element_type | solution.py:205
  (174 shorter events, 56.4 us)
Async XLA Ops:
  0.6 12.8 %copy-start = (f32[4,7]{1,0:T(4,128)S(1)}, f32[4,7]{1,0:T(4,128)}, u32[]{:S(2)}) copy-start(f32[4,7]{1,0:T(4,128)} %param.17) | copy-start | bytes 340
  1.3 12.4 %copy-start.7 = (bf16[1,256,512]{2,1,0:T(8,128)(2,1)S(1)}, bf16[1,256,512]{2,1,0:T(8,128)(2,1)}, u32[]{:S(2)}) copy-start(bf16[1,256,512]{2,1,0:T(8,128)(2,1)} %param.11) | copy-start | bytes 786436
  1.3 31.4 %collective-permute-start.7 = (bf16[2,2]{1,0:T(2,128)(2,1)S(1)}, bf16[2,2]{1,0:T(2,128)(2,1)S(1)}, u32[]{:S(2)}, u32[]{:S(2)}) collective-permute-start(bf16[2,2]{1,0:T(2,128)(2,1)S(1)} %convert_bitcast_fusion), channel_id=1, source_target_pairs={{4,0},{5,1},{6,2},{7,3},{12,8},{13,9},{14,10},{15,11},{20,16},{21,... | collective-permute-start | bytes 32 | tf_op jit(solution)/shard_map/ppermute | solution.py:16
  2.8 32.0 %collective-permute-start.3 = (bf16[2,2]{1,0:T(2,128)(2,1)S(1)}, bf16[2,2]{1,0:T(2,128)(2,1)S(1)}, u32[]{:S(2)}, u32[]{:S(2)}) collective-permute-start(bf16[2,2]{1,0:T(2,128)(2,1)S(1)} %convert_bitcast_fusion), channel_id=1, source_target_pairs={{2,0},{3,1},{4,2},{5,3},{6,4},{7,5},{10,8},{11,9},{12,10},{13,11},... | collective-permute-start | bytes 32 | tf_op jit(solution)/shard_map/ppermute | solution.py:16
  6.9 60.2 %collective-permute-start.8 = (bf16[256,512]{0,1:T(8,128)(2,1)}, bf16[256,512]{0,1:T(8,128)(2,1)}, u32[]{:S(2)}, u32[]{:S(2)}) collective-permute-start(bf16[256,512]{0,1:T(8,128)(2,1)} %bitcast.8), channel_id=1, source_target_pairs={{4,0},{5,1},{6,2},{7,3},{12,8},{13,9},{14,10},{15,11},{20,16},{21,... | collective-permute-start | bytes 786440 | tf_op jit(solution)/shard_map/ppermute | solution.py:16
  8.2 51.5 %collective-permute-start.4 = (bf16[256,512]{0,1:T(8,128)(2,1)}, bf16[256,512]{0,1:T(8,128)(2,1)}, u32[]{:S(2)}, u32[]{:S(2)}) collective-permute-start(bf16[256,512]{0,1:T(8,128)(2,1)} %bitcast.8), channel_id=1, source_target_pairs={{2,0},{3,1},{4,2},{5,3},{6,4},{7,5},{10,8},{11,9},{12,10},{13,11},... | collective-permute-start | bytes 786440 | tf_op jit(solution)/shard_map/ppermute | solution.py:16
  10.1 66.4 %collective-permute-start = (bf16[256,512]{0,1:T(8,128)(2,1)}, bf16[256,512]{0,1:T(8,128)(2,1)}, u32[]{:S(2)}, u32[]{:S(2)}) collective-permute-start(bf16[256,512]{0,1:T(8,128)(2,1)} %bitcast.8), channel_id=1, source_target_pairs={{1,0},{2,1},{3,2},{4,3},{5,4},{6,5},{7,6},{9,8},{10,9},{11,10},{12... | collective-permute-start | bytes 786440 | tf_op jit(solution)/shard_map/ppermute | solution.py:16
  12.1 1.3 copy-start.34
  15.7 2.0 %copy-start.2 = (bf16[1,256,512]{1,2,0:T(8,128)(2,1)}, bf16[1,256,512]{1,2,0:T(8,128)(2,1)S(1)}, u32[]{:S(2)}) copy-start(bf16[1,256,512]{1,2,0:T(8,128)(2,1)S(1)} %copy.255) | copy-start | bytes 786436
  18.4 2.3 %copy-start.22 = (bf16[256,4,128]{2,1,0:T(4,128)(2,1)S(1)}, bf16[256,4,128]{2,1,0:T(4,128)(2,1)}, u32[]{:S(2)}) copy-start(bf16[256,4,128]{2,1,0:T(4,128)(2,1)} %reshape.770) | copy-start | bytes 786436
  20.6 1.6 copy-start.3
  32.3 4.6 %copy-start.6 = (bf16[1,256,512]{2,1,0:T(8,128)(2,1)S(1)}, bf16[1,256,512]{2,1,0:T(8,128)(2,1)}, u32[]{:S(2)}) copy-start(bf16[1,256,512]{2,1,0:T(8,128)(2,1)} %param.12) | copy-start | bytes 786436
  33.3 31.8 %collective-permute-start.9 = (bf16[256,512]{0,1:T(8,128)(2,1)S(1)}, bf16[256,512]{0,1:T(8,128)(2,1)}, u32[]{:S(2)}, u32[]{:S(2)}) collective-permute-start(bf16[256,512]{0,1:T(8,128)(2,1)S(1)} %bitcast.193), channel_id=1, source_target_pairs={{4,0},{5,1},{6,2},{7,3},{12,8},{13,9},{14,10},{15,11},{20,16},{21,... | collective-permute-start | bytes 786440 | tf_op jit(solution)/shard_map/ppermute | solution.py:16
  34.8 5.5 %copy-start.30 = (s32[2]{0:T(128)}, s32[2]{0:T(128)S(1)}, u32[]{:S(2)}) copy-start(s32[2]{0:T(128)S(1)} %get-tuple-element.15) | copy-start | bytes 28
  34.8 20.9 %collective-permute-start.5 = (bf16[256,512]{0,1:T(8,128)(2,1)S(1)}, bf16[256,512]{0,1:T(8,128)(2,1)}, u32[]{:S(2)}, u32[]{:S(2)}) collective-permute-start(bf16[256,512]{0,1:T(8,128)(2,1)S(1)} %bitcast.194), channel_id=1, source_target_pairs={{2,0},{3,1},{4,2},{5,3},{6,4},{7,5},{10,8},{11,9},{12,10},{13,11},... | collective-permute-start | bytes 786440 | tf_op jit(solution)/shard_map/ppermute | solution.py:16
  36.9 4.1 %copy-start.32 = (s32[2]{0:T(128)}, s32[2]{0:T(128)S(1)}, u32[]{:S(2)}) copy-start(s32[2]{0:T(128)S(1)} %get-tuple-element.11) | copy-start | bytes 28
  55.6 17.7 %collective-permute-start.1 = (bf16[256,512]{0,1:T(8,128)(2,1)S(1)}, bf16[256,512]{0,1:T(8,128)(2,1)S(1)}, u32[]{:S(2)}, u32[]{:S(2)}) collective-permute-start(bf16[256,512]{0,1:T(8,128)(2,1)S(1)} %bitcast.195), channel_id=1, source_target_pairs={{1,0},{2,1},{3,2},{4,3},{5,4},{6,5},{7,6},{9,8},{10,9},{11,10},{12... | collective-permute-start | bytes 786440 | tf_op jit(solution)/shard_map/ppermute | solution.py:16
  59.7 4.1 %copy-start.17 = (f32[2,4,128,128]{2,3,1,0:T(8,128)}, f32[2,4,128,128]{2,3,1,0:T(8,128)S(1)}, u32[]{:S(2)}) copy-start(f32[2,4,128,128]{2,3,1,0:T(8,128)S(1)} %fusion.19) | copy-start | bytes 1572868
  67.1 4.0 %copy-start.19 = (f32[2,4,128,128]{2,3,1,0:T(8,128)}, f32[2,4,128,128]{2,3,1,0:T(8,128)S(1)}, u32[]{:S(2)}) copy-start(f32[2,4,128,128]{2,3,1,0:T(8,128)S(1)} %fusion.16) | copy-start | bytes 1572868
  73.7 2.8 %copy-start.15 = (f32[4,256,256]{2,1,0:T(8,128)}, f32[4,256,256]{2,1,0:T(8,128)S(1)}, u32[]{:S(2)}) copy-start(f32[4,256,256]{2,1,0:T(8,128)S(1)} %fusion) | copy-start | bytes 3145732
  73.7 1.4 copy-start.20
  73.7 1.7 copy-start.25
  76.6 1.6 copy-start.1
  102.7 8.1 %copy-start.16 = (f32[4,256,256]{2,1,0:T(8,128)S(1)}, f32[4,256,256]{2,1,0:T(8,128)}, u32[]{:S(2)}) copy-start(f32[4,256,256]{2,1,0:T(8,128)} %copy-done.15) | copy-start | bytes 3145732
  104.9 5.9 %copy-start.38 = (f32[4,256,128]{1,2,0:T(8,128)S(1)}, f32[4,256,128]{1,2,0:T(8,128)}, u32[]{:S(2)}) copy-start(f32[4,256,128]{1,2,0:T(8,128)} %fusion.27) | copy-start | bytes 1572868
  105.8 54.5 %collective-permute-start.10 = (f32[256,512]{1,0:T(8,128)}, f32[256,512]{1,0:T(8,128)}, u32[]{:S(2)}, u32[]{:S(2)}) collective-permute-start(f32[256,512]{1,0:T(8,128)} %bitcast.181), channel_id=1, source_target_pairs={{0,4},{1,5},{2,6},{3,7},{8,12},{9,13},{10,14},{11,15},{16,20},{17,... | collective-permute-start | bytes 1572872 | tf_op jit(solution)/shard_map/ppermute | solution.py:16
  108.9 51.4 %collective-permute-start.6 = (f32[256,512]{1,0:T(8,128)}, f32[256,512]{1,0:T(8,128)}, u32[]{:S(2)}, u32[]{:S(2)}) collective-permute-start(f32[256,512]{1,0:T(8,128)} %bitcast.182), channel_id=1, source_target_pairs={{0,2},{1,3},{2,4},{3,5},{4,6},{5,7},{8,10},{9,11},{10,12},{11,13},... | collective-permute-start | bytes 1572872 | tf_op jit(solution)/shard_map/ppermute | solution.py:16
  119.2 2.1 %copy-start.35 = (s32[2,2]{1,0:T(2,128)S(1)}, s32[2,2]{1,0:T(2,128)}, u32[]{:S(2)}) copy-start(s32[2,2]{1,0:T(2,128)} %copy-done.34) | copy-start | bytes 52
  120.3 37.9 %copy-start.10 = (f32[2,128,512]{2,1,0:T(8,128)S(1)}, f32[2,128,512]{2,1,0:T(8,128)}, u32[]{:S(2)}) copy-start(f32[2,128,512]{2,1,0:T(8,128)} %copy.225) | copy-start | bytes 1572868
  120.3 37.9 %copy-start.12 = (f32[1,256,512]{2,1,0:T(8,128)S(1)}, f32[1,256,512]{2,1,0:T(8,128)}, u32[]{:S(2)}) copy-start(f32[1,256,512]{2,1,0:T(8,128)} %copy.221) | copy-start | bytes 1572868
  156.2 10.7 %collective-permute-start.2 = (f32[256,512]{1,0:T(8,128)}, f32[256,512]{1,0:T(8,128)S(1)}, u32[]{:S(2)}, u32[]{:S(2)}) collective-permute-start(f32[256,512]{1,0:T(8,128)} %copy.180), channel_id=1, source_target_pairs={{0,1},{1,2},{2,3},{3,4},{4,5},{5,6},{6,7},{8,9},{9,10},{10,11},{11... | collective-permute-start | bytes 1572872 | tf_op jit(solution)/shard_map/ppermute | solution.py:16
  159.5 7.5 %copy-start.14 = (f32[256,512]{1,0:T(8,128)S(1)}, f32[256,512]{1,0:T(8,128)}, u32[]{:S(2)}) copy-start(f32[256,512]{1,0:T(8,128)} %copy.181) | copy-start | bytes 1572868
  (18 other events, 16.0 us)
